TPU v7x, 512 devices: a whole 4x8x8 slice. The times are simulated.
512 devices in a mesh: dom: 128 (over z, y, core), grp: 4 (over x).
Axes of the slice: x: 4, y: 8, z: 8, core: 2. Of those that a mesh axis runs over, the one named last changes fastest.
Arguments:
- source_emb: float32 [400, 65536], P(None, ('dom', 'grp')), may hold values from -2.5 to 2.5
- source_state: float32 [65536], P(('dom', 'grp')), may hold values from 0.005 to 0.1
- dest_emb: float32 [400, 65536], P(None, ('dom', 'grp')), may hold values from -2.5 to 2.5
- dest_state: float32 [65536], P(('dom', 'grp')), may hold values from 0.005 to 0.1
- relations: float32 [400, 768], replicated, may hold values from -4 to 4
- relation_state: float32 [768], replicated, may hold values from 1 to 30
- partner: int32 [128, 4], P('dom', 'grp'), may hold values from 0 to 127, as said below
- edge_count: int32 [128, 4], P('dom', 'grp'), may hold values from 1 to 1024, as said below
- source_rows: int32 [128, 4, 1024], P('dom', 'grp'), may hold values from 0 to 127
- target_rows: int32 [128, 4, 1024], P('dom', 'grp'), may hold values from 0 to 127
- relation_index: int32 [128, 4, 1024], P('dom', 'grp'), may hold values from 0 to 767
- negative_rows: int32 [128, 4, 2048], P('dom', 'grp'), may hold values from 0 to 127
Outputs:
- source_out: float32 [400, 65536], P(None, ('dom', 'grp'))
- source_state_out: float32 [65536], P(('dom', 'grp'))
- dest_out: float32 [400, 65536], P(None, ('dom', 'grp'))
- dest_state_out: float32 [65536], P(('dom', 'grp'))
- relations_out: float32 [400, 768], replicated
- relation_state_out: float32 [768], replicated
Inputs may be any that keep to these rules, and one draw needn't show every extreme that they name: For each grp index g, partner[:, g] is a permutation of 0 .. 127. `edge_count`: some device has all 1024 edges live.
All inputs are finite; a program needn't handle non-finite values.
Results may differ from a plain program's by a relative error of at most 0.0013.
The roundings to bfloat16 on the way count: a program that leaves them out, or rounds other values in their place, can miss the bound.
Values sent between devices are 32-bit elements; how exact they have to be, the bound alone decides.
No kernel may reach another device: no remote copies, remote signals or barrier semaphores. Data moves between devices by JAX's collectives and lax.ppermute only.
A program may use at most 64 MiB of HBM per device.

v0:
```python
import jax
import jax.numpy as jnp
from jax import lax
from jax.sharding import PartitionSpec as P

SPAN = 512
SPANS = 2
NEG = 1024
EDGES = 1024
learn_rate = 0.3
epsilon = 1e-08


def passed_along(value, axis, steps):
    count = lax.axis_size(axis)
    pairs = [(source, (source + steps) % count) for source in range(count)]
    return lax.ppermute(value, axis, pairs)


def adagrad(param, state, grad):
    new_state = state + jnp.mean(grad * grad, axis=0)
    return (param - learn_rate * grad / (jnp.sqrt(new_state) + epsilon), new_state)


def contract_last(left, right):
    return lax.dot_general(
        left, right, (((1,), (1,)), ((), ())), preferred_element_type=jnp.float32
    )


def selector(count, rows):
    return (jnp.arange(count, dtype=jnp.int32)[:, None] == rows[None, :]).astype(jnp.bfloat16)


def train_block(
    source, source_acc, target, target_acc, relation_bf, rows_s, rows_t, rows_r, rows_n, live
):
    width = source.shape[0]
    half = width // 2
    block = source.shape[1]
    pick_source = selector(block, rows_s)
    pick_target = selector(block, rows_t)
    pick_noise = selector(block, rows_n)
    pick_relation = selector(relation_bf.shape[1], rows_r)
    source_bf = source.astype(jnp.bfloat16)
    target_bf = target.astype(jnp.bfloat16)
    subject = jnp.dot(source_bf, pick_source, preferred_element_type=jnp.float32)
    operator = jnp.dot(relation_bf, pick_relation, preferred_element_type=jnp.float32)
    objects = jnp.dot(target_bf, pick_target, preferred_element_type=jnp.float32)
    noise = jnp.dot(target_bf, pick_noise, preferred_element_type=jnp.float32).astype(jnp.bfloat16)
    subject_re, subject_im = (subject[:half], subject[half:])
    operator_re, operator_im = (operator[:half], operator[half:])
    query = jnp.concatenate(
        [
            subject_re * operator_re - subject_im * operator_im,
            subject_re * operator_im + subject_im * operator_re,
        ],
        0,
    )
    positive = jnp.sum(query * objects, axis=0)
    query_bf = query.astype(jnp.bfloat16)
    negative = lax.dot_general(
        query_bf, noise, (((0,), (0,)), ((), ())), preferred_element_type=jnp.float32
    )
    grad_pos = -jax.nn.sigmoid(-positive) * live
    grad_neg = (jax.nn.sigmoid(negative) * (live[:, None] / NEG)).astype(jnp.bfloat16)
    grad_query = grad_pos[None, :] * objects + contract_last(noise, grad_neg)
    grad_objects = grad_pos[None, :] * query
    grad_noise = jnp.dot(query_bf, grad_neg, preferred_element_type=jnp.float32)
    query_gre, query_gim = (grad_query[:half], grad_query[half:])
    grad_subject = jnp.concatenate(
        [
            query_gre * operator_re + query_gim * operator_im,
            query_gim * operator_re - query_gre * operator_im,
        ],
        0,
    )
    grad_operator = jnp.concatenate(
        [
            query_gre * subject_re + query_gim * subject_im,
            query_gim * subject_re - query_gre * subject_im,
        ],
        0,
    )
    grad_source = contract_last(grad_subject.astype(jnp.bfloat16), pick_source)
    grad_target = contract_last(grad_objects.astype(jnp.bfloat16), pick_target)
    grad_target = grad_target + contract_last(grad_noise.astype(jnp.bfloat16), pick_noise)
    grad_local = contract_last(grad_operator.astype(jnp.bfloat16), pick_relation)
    new_source, new_source_acc = adagrad(source, source_acc, grad_source)
    new_target, new_target_acc = adagrad(target, target_acc, grad_target)
    return (new_source, new_source_acc, new_target, new_target_acc, grad_local)


def relation_step(relations, relation_state, grad_local):
    total = lax.psum(grad_local, ("dom", "grp"))
    return adagrad(relations, relation_state, total)


def local(
    source_emb,
    source_state,
    dest_emb,
    dest_state,
    relations,
    relation_state,
    partner,
    edge_count,
    source_rows,
    target_rows,
    relation_index,
    negative_rows,
):
    width = source_emb.shape[0]
    block = source_emb.shape[1]
    members = lax.axis_size("dom")
    piece = block // members
    cargo = jnp.concatenate([dest_emb, dest_state[None, :]], 0)
    cargo = passed_along(cargo, "grp", 1)
    partners = lax.all_gather(partner[0], "dom", axis=0, tiled=True)
    spread = lax.all_to_all(
        cargo.reshape(width + 1, members, piece), "dom", split_axis=1, concat_axis=1, tiled=True
    )
    spread = jnp.take(spread, partners, axis=1)
    arrived = lax.all_to_all(spread, "dom", split_axis=1, concat_axis=1, tiled=True).reshape(
        width + 1, block
    )
    target = arrived[:width]
    target_acc = arrived[width]
    source = source_emb
    source_acc = source_state
    live_all = (jnp.arange(EDGES, dtype=jnp.int32) < edge_count[0, 0]).astype(jnp.float32)
    for step in range(SPANS):
        first = step * SPAN
        first_neg = step * NEG
        relation_bf = relations.astype(jnp.bfloat16)
        source, source_acc, target, target_acc, grad_local = train_block(
            source,
            source_acc,
            target,
            target_acc,
            relation_bf,
            source_rows[0, 0, first : first + SPAN],
            target_rows[0, 0, first : first + SPAN],
            relation_index[0, 0, first : first + SPAN],
            negative_rows[0, 0, first_neg : first_neg + NEG],
            live_all[first : first + SPAN],
        )
        relations, relation_state = relation_step(relations, relation_state, grad_local)
    cargo = jnp.concatenate([target, target_acc[None, :]], 0).reshape(width + 1, members, piece)
    collected = lax.all_to_all(cargo, "dom", split_axis=1, concat_axis=1, tiled=True)
    inverse = (
        jnp.zeros((members,), jnp.int32).at[partners].set(jnp.arange(members, dtype=jnp.int32))
    )
    collected = jnp.take(collected, inverse, axis=1)
    returned = lax.all_to_all(collected, "dom", split_axis=1, concat_axis=1, tiled=True).reshape(
        width + 1, block
    )
    settled = passed_along(returned, "grp", -1)
    return (source, source_acc, settled[:width], settled[width], relations, relation_state)


def solution(mesh):
    in_specs = (
        P(None, ("dom", "grp")),
        P(("dom", "grp")),
        P(None, ("dom", "grp")),
        P(("dom", "grp")),
        P(),
        P(),
        P("dom", "grp"),
        P("dom", "grp"),
        P("dom", "grp", None),
        P("dom", "grp", None),
        P("dom", "grp", None),
        P("dom", "grp", None),
    )
    out_specs = (
        P(None, ("dom", "grp")),
        P(("dom", "grp")),
        P(None, ("dom", "grp")),
        P(("dom", "grp")),
        P(),
        P(),
    )
    return jax.shard_map(local, mesh=mesh, in_specs=in_specs, out_specs=out_specs, check_vma=False)
```

profile of v0, /device:TPU:23, one launch (start us, length us, event | category | flops | bytes accessed | tf_op | source)
XLA Modules:
  0.0 705.2 jit_solution(11849376523727967690)
XLA Ops:
  7.2 1.1 pad_maximum_fusion.2
  8.2 2.1 collective-permute-start
  11.0 1.3 dynamic-slice
  13.0 27.1 %all-reduce = s32[128]{0:T(128)S(1)} all-reduce(s32[128]{0:T(128)S(1)} %bitcast_dynamic-update-slice_fusion), channel_id=2, replica_groups=mesh['dom'=128,'grp'=4] {'dom'}, use_global_device_ids=true, to_apply=%add | all-reduce | flops 128 | bytes 1024 | tf_op jit(solution)/shard_map/all_gather | solution.py:119
  40.0 0.7 fusion.78
  40.7 0.7 fusion.77
  41.4 0.7 fusion.79
  42.1 0.7 fusion.76
  42.9 1.0 scatter_custom_fusion
  43.8 1.2 convolution_bitcast_fusion
  45.1 0.8 copy.35
  45.9 11.1 %all-to-all-start = ((f32[401,128,1]{0,2,1:T(1,128)}), f32[401,128,1]{0,2,1:T(1,128)S(1)}, u32[]{:S(2)}, u32[]{:S(2)}) async-start(f32[401,128,1]{0,2,1:T(1,128)} %copy.35), calls=%async_computation | async-start | bytes 524288 | tf_op jit(solution)/shard_map/all_to_all | solution.py:120
  58.2 11.9 %all-to-all-done = f32[401,128,1]{0,2,1:T(1,128)S(1)} async-done(((f32[401,128,1]{0,2,1:T(1,128)}), f32[401,128,1]{0,2,1:T(1,128)S(1)}, u32[]{:S(2)}, u32[]{:S(2)}) %all-to-all-start) | async-done | bytes 205344 | tf_op jit(solution)/shard_map/all_to_all | solution.py:120
  70.1 0.8 gather_fusion
  70.9 1.0 copy.38
  71.9 8.8 %all-to-all-start.1 = ((f32[401,128,1]{0,2,1:T(1,128)}), f32[401,128,1]{0,2,1:T(1,128)}, u32[]{:S(2)}, u32[]{:S(2)}) async-start(f32[401,128,1]{0,2,1:T(1,128)} %copy.38), calls=%async_computation.1 | async-start | bytes 524288 | tf_op jit(solution)/shard_map/all_to_all | solution.py:124
  81.0 0.9 multiply_subtract_fusion.1
  81.9 11.6 %all-to-all-done.1 = f32[401,128,1]{0,2,1:T(1,128)} async-done(((f32[401,128,1]{0,2,1:T(1,128)}), f32[401,128,1]{0,2,1:T(1,128)}, u32[]{:S(2)}, u32[]{:S(2)}) %all-to-all-start.1) | async-done | bytes 205344 | tf_op jit(solution)/shard_map/all_to_all | solution.py:124
  93.5 1.1 copy.47
  95.6 1.2 multiply_reduce_fusion.3
  96.8 1.0 fusion.31
  97.8 2.0 multiply_convert_fusion.1
  99.8 2.9 multiply_reduce_fusion.6
  102.7 2.3 convolution_add_fusion.1
  105.4 1.6 fusion.2
  107.3 2.7 slice_reduce_fusion
  110.1 1.3 convolution_convert_fusion.1
  111.7 264.1 %all-reduce.4.cloned.1.call-done = f32[400,768]{1,0:T(8,128)} async-done(((f32[400,768]{1,0:T(8,128)}), f32[400,768]{1,0:T(8,128)}) %all-reduce.4.cloned.1.call-update) | async-done | bytes 1228816 | tf_op jit(solution)/shard_map/psum | solution.py:95
  375.8 1.5 multiply_reduce_fusion.1
  379.0 1.2 multiply_reduce_fusion.2
  380.2 1.0 fusion.32
  381.2 2.0 multiply_convert_fusion
  383.2 3.0 multiply_reduce_fusion.4
  386.2 2.4 convolution_add_fusion
  388.6 1.3 add_convert_fusion
  390.0 0.8 copy.40
  390.8 9.6 %all-to-all-start.2 = ((f32[401,128,1]{0,2,1:T(1,128)}), f32[401,128,1]{0,2,1:T(1,128)S(1)}, u32[]{:S(2)}, u32[]{:S(2)}) async-start(f32[401,128,1]{0,2,1:T(1,128)} %copy.40), calls=%async_computation.2 | async-start | bytes 524288 | tf_op jit(solution)/shard_map/all_to_all | solution.py:150
  400.5 2.6 fusion
  403.9 9.6 %all-to-all-done.2 = f32[401,128,1]{0,2,1:T(1,128)S(1)} async-done(((f32[401,128,1]{0,2,1:T(1,128)}), f32[401,128,1]{0,2,1:T(1,128)S(1)}, u32[]{:S(2)}, u32[]{:S(2)}) %all-to-all-start.2) | async-done | bytes 205344 | tf_op jit(solution)/shard_map/all_to_all | solution.py:150
  413.5 0.8 gather_fusion.1
  414.4 1.0 copy.43
  415.3 7.7 %all-to-all-start.3 = ((f32[401,128,1]{0,2,1:T(1,128)}), f32[401,128,1]{0,2,1:T(1,128)S(1)}, u32[]{:S(2)}, u32[]{:S(2)}) async-start(f32[401,128,1]{0,2,1:T(1,128)} %copy.43), calls=%async_computation.3 | async-start | bytes 524288 | tf_op jit(solution)/shard_map/all_to_all | solution.py:155
  423.1 0.7 divide_subtract_fusion.3
  423.8 261.1 %all-reduce.6.cloned.1.call-done = f32[400,768]{1,0:T(8,128)} async-done(((f32[400,768]{1,0:T(8,128)}), f32[400,768]{1,0:T(8,128)}) %all-reduce.6.cloned.1.call-update) | async-done | bytes 1228816 | tf_op jit(solution)/shard_map/psum | solution.py:95
  684.9 1.4 multiply_reduce_fusion
  687.0 2.3 collective-permute-start.1
  689.3 2.6 divide_subtract_fusion
  691.9 5.2 collective-permute-done.1
  (83 shorter events, 8.2 us)
Async XLA Ops:
  7.2 50.5 %copy-start = (f32[400,768]{1,0:T(8,128)S(1)}, f32[400,768]{1,0:T(8,128)}, u32[]{:S(2)}) copy-start(f32[400,768]{1,0:T(8,128)} %param.18) | copy-start | bytes 3686404
  8.2 36.8 %collective-permute-start = (f32[401,128]{1,0:T(8,128)S(1)}, f32[401,128]{1,0:T(8,128)S(1)}, u32[]{:S(2)}, u32[]{:S(2)}) collective-permute-start(f32[401,128]{1,0:T(8,128)S(1)} %pad_maximum_fusion.2), channel_id=1, source_target_pairs={{0,1},{1,2},{2,3},{3,0},{4,5},{5,6},{6,7},{7,4},{8,9},{9,10},{10,1... | collective-permute-start | bytes 615944 | tf_op jit(solution)/shard_map/ppermute | solution.py:17
  45.9 24.2 %all-to-all-start = ((f32[401,128,1]{0,2,1:T(1,128)}), f32[401,128,1]{0,2,1:T(1,128)S(1)}, u32[]{:S(2)}, u32[]{:S(2)}) async-start(f32[401,128,1]{0,2,1:T(1,128)} %copy.35), calls=%async_computation | async-start | bytes 524288 | tf_op jit(solution)/shard_map/all_to_all | solution.py:120
  71.9 21.6 %all-to-all-start.1 = ((f32[401,128,1]{0,2,1:T(1,128)}), f32[401,128,1]{0,2,1:T(1,128)}, u32[]{:S(2)}, u32[]{:S(2)}) async-start(f32[401,128,1]{0,2,1:T(1,128)} %copy.38), calls=%async_computation.1 | async-start | bytes 524288 | tf_op jit(solution)/shard_map/all_to_all | solution.py:124
  80.7 295.1 %all-reduce.4.cloned.1.call-start = ((), (), s32[]{:S(2)}) async-start(), calls=%async_computation.4 | async-start | bytes 2457600 | tf_op jit(solution)/shard_map/psum | solution.py:95
  94.6 1.0 copy-start.8
  95.0 2.8 copy-start.5
  106.9 3.1 copy-start.16
  107.0 3.1 copy-start.19
  107.0 4.4 copy-start.6
  107.3 4.1 copy-start.11
  111.4 265.9 %copy-start.18 = (f32[768]{0:T(1024)S(1)}, f32[768]{0:T(1024)}, u32[]{:S(2)}) copy-start(f32[768]{0:T(1024)} %param.19) | copy-start | bytes 9220
  375.8 1.7 copy-start.1
  378.1 0.9 copy-start.2
  378.3 2.9 copy-start.9
  378.3 2.9 copy-start.10
  379.0 2.2 copy-start.4
  386.2 2.4 copy-start.3
  388.6 1.3 copy-start.17
  389.9 10.5 %copy-start.15 = (bf16[200,512]{1,0:T(8,128)(2,1)S(1)}, bf16[200,512]{1,0:T(8,128)(2,1)}, u32[]{:S(2)}) copy-start(bf16[200,512]{1,0:T(8,128)(2,1)} %get-tuple-element.29) | copy-start | bytes 614404
  390.8 22.6 %all-to-all-start.2 = ((f32[401,128,1]{0,2,1:T(1,128)}), f32[401,128,1]{0,2,1:T(1,128)S(1)}, u32[]{:S(2)}, u32[]{:S(2)}) async-start(f32[401,128,1]{0,2,1:T(1,128)} %copy.40), calls=%async_computation.2 | async-start | bytes 524288 | tf_op jit(solution)/shard_map/all_to_all | solution.py:150
  400.4 284.5 %all-reduce.6.cloned.1.call-start = ((), (), s32[]{:S(2)}) async-start(), calls=%async_computation.5 | async-start | bytes 2457600 | tf_op jit(solution)/shard_map/psum | solution.py:95
  400.4 2.6 copy-start.13
  400.4 2.6 copy-start.14
  414.2 8.8 %copy-start.7 = (f32[400,128]{1,0:T(8,128)S(1)}, f32[400,128]{1,0:T(8,128)}, u32[]{:S(2)}) copy-start(f32[400,128]{1,0:T(8,128)} %param.14) | copy-start | bytes 614404
  414.2 8.8 %copy-start.12 = (f32[400,128]{1,0:T(8,128)S(1)}, f32[400,128]{1,0:T(8,128)}, u32[]{:S(2)}) copy-start(f32[400,128]{1,0:T(8,128)} %copy-done.11) | copy-start | bytes 614404
  415.3 271.6 %all-to-all-start.3 = ((f32[401,128,1]{0,2,1:T(1,128)}), f32[401,128,1]{0,2,1:T(1,128)S(1)}, u32[]{:S(2)}, u32[]{:S(2)}) async-start(f32[401,128,1]{0,2,1:T(1,128)} %copy.43), calls=%async_computation.3 | async-start | bytes 524288 | tf_op jit(solution)/shard_map/all_to_all | solution.py:155
  687.0 10.1 %collective-permute-start.1 = (f32[401,128]{1,0:T(8,128)S(1)}, f32[401,128]{1,0:T(8,128)S(1)}, u32[]{:S(2)}, u32[]{:S(2)}) collective-permute-start(f32[401,128]{1,0:T(8,128)S(1)} %bitcast.84), channel_id=1, source_target_pairs={{0,3},{1,0},{2,1},{3,2},{4,7},{5,4},{6,5},{7,6},{8,11},{9,8},{10,9... | collective-permute-start | bytes 615944 | tf_op jit(solution)/shard_map/ppermute | solution.py:17
Sparse Core Ops, SparseCore 0:
  107.1 268.6 all-reduce.3
  407.7 277.1 all-reduce.5
where the time goes:
time: 706 us; the launch traced here: 705 us
  waiting for transfers between devices  564 us (80%)
  starting transfers between devices  41.8 us (6%)
  matrix products  27.9 us (4%)
  blocking collectives  27.1 us (4%)
  local copies, waits for them, and re-layouts  17.5 us (2%)
  between operations  15.8 us (2%)
  other arithmetic  11.5 us (2%)
    psum x2, waiting for transfers between devices, relation_step(): total = lax.psum(grad_local, ('dom', 'grp'))  525 us
    all_gather x1, blocking collectives, local(): partners = lax.all_gather(partner[0], 'dom', axis=0, tiled=True)  27.1 us
    dot_general x10, matrix products, contract_last(): lax.dot_general(left, right, (((1,), (1,)), ((), ())), preferred_element_...  17.3 us
  transfers between devices with their start and end apart: 8, of which 6 were waited for; matrix products, arithmetic and copies ran while one was open for 3% of the time, Pallas kernels for 0%

commit v1 on v0

--- a/solution.py
+++ b/solution.py
@@ -117,8 +117,16 @@
     cargo = jnp.concatenate([dest_emb, dest_state[None, :]], 0)
     cargo = passed_along(cargo, "grp", 1)
     partners = lax.all_gather(partner[0], "dom", axis=0, tiled=True)
-    spread = lax.all_to_all(
-        cargo.reshape(width + 1, members, piece), "dom", split_axis=1, concat_axis=1, tiled=True
+    spread = jnp.concatenate(
+        lax.all_to_all(
+            jnp.stack(
+                jnp.split(cargo.reshape(width + 1, members, piece), lax.axis_size("dom"), axis=1)
+            ),
+            "dom",
+            0,
+            0,
+        ),
+        axis=1,
     )
     spread = jnp.take(spread, partners, axis=1)
     arrived = lax.all_to_all(spread, "dom", split_axis=1, concat_axis=1, tiled=True).reshape(

time: 706 us -> 806 us (1.14); the launches traced: 705 us -> 796 us
  local copies, waits for them, and re-layouts: 17.5 us -> 108 us
    unnamed x44 -> x173, local copies, waits for them, and re-layouts: 4.52 us -> 78 us
    split x0 -> x7, local copies, waits for them, and re-layouts: none -> 16.8 us  [local(): jnp.split(cargo.reshape(width + 1, members, piece), lax.axis_size('dom'),...]
where the time goes in v1:
time: 806 us; the launch traced here: 796 us
  waiting for transfers between devices  562 us (70%)
  local copies, waits for them, and re-layouts  108 us (13%)
  starting transfers between devices  41.8 us (5%)
  matrix products  28.6 us (4%)
  blocking collectives  27.1 us (3%)
  between operations  16.1 us (2%)
  other arithmetic  13 us (2%)
    psum x2, waiting for transfers between devices, relation_step(): total = lax.psum(grad_local, ('dom', 'grp'))  524 us
    unnamed x173, local copies, waits for them, and re-layouts  78 us
    all_gather x1, blocking collectives, local(): partners = lax.all_gather(partner[0], 'dom', axis=0, tiled=True)  27.1 us
    dot_general x10, matrix products, contract_last(): lax.dot_general(left, right, (((1,), (1,)), ((), ())), preferred_element_...  17.9 us
    split x7, local copies, waits for them, and re-layouts, local(): jnp.split(cargo.reshape(width + 1, members, piece), lax.axis_size('dom'),...  16.8 us
  transfers between devices with their start and end apart: 8, of which 6 were waited for; matrix products, arithmetic and copies ran while one was open for 3% of the time, Pallas kernels for 0%

profile of v1, /device:TPU:23, one launch (start us, length us, event | category | flops | bytes accessed | tf_op | source)
XLA Modules:
  0.0 796.2 jit_solution(15902560031424962784)
XLA Ops:
  7.2 1.0 pad_maximum_fusion.2
  8.1 2.1 collective-permute-start
  10.9 1.3 dynamic-slice
  12.8 27.1 %all-reduce = s32[128]{0:T(128)S(1)} all-reduce(s32[128]{0:T(128)S(1)} %bitcast_dynamic-update-slice_fusion), channel_id=2, replica_groups=mesh['dom'=128,'grp'=4] {'dom'}, use_global_device_ids=true, to_apply=%add | all-reduce | flops 128 | bytes 1024 | tf_op jit(solution)/shard_map/all_gather | solution.py:119
  42.7 1.0 scatter_custom_fusion
  43.7 1.2 convolution_bitcast_fusion
  45.0 1.8 slice_reduce_fusion.114
  46.7 2.4 slice_reduce_fusion.19
  49.2 2.4 slice_reduce_fusion.76
  51.6 2.4 slice_reduce_fusion.38
  54.0 2.4 slice_reduce_fusion.57
  56.5 2.9 slice_reduce_fusion
  59.4 2.4 slice_reduce_fusion.95
  135.9 11.1 %all-to-all-start = ((f32[128,401,1,1]{1,3,2,0:T(1,128)}), f32[128,401,1,1]{1,3,2,0:T(1,128)S(1)}, u32[]{:S(2)}, u32[]{:S(2)}) async-start(f32[128,401,1,1]{1,3,2,0:T(1,128)} %constant_dynamic-update-slice_fusion), calls=%async_computation | async-start | bytes 524288 | tf_op jit(solution)/shard_map/all_to_all | solution.py:121
  148.2 11.9 %all-to-all-done = f32[128,401,1,1]{1,3,2,0:T(1,128)S(1)} async-done(((f32[128,401,1,1]{1,3,2,0:T(1,128)}), f32[128,401,1,1]{1,3,2,0:T(1,128)S(1)}, u32[]{:S(2)}, u32[]{:S(2)}) %all-to-all-start) | async-done | bytes 205344 | tf_op jit(solution)/shard_map/all_to_all | solution.py:121
  160.9 1.0 copy.159
  161.9 8.8 %all-to-all-start.1 = ((f32[401,128,1]{0,2,1:T(1,128)}), f32[401,128,1]{0,2,1:T(1,128)}, u32[]{:S(2)}, u32[]{:S(2)}) async-start(f32[401,128,1]{0,2,1:T(1,128)} %copy.159), calls=%async_computation.1 | async-start | bytes 524288 | tf_op jit(solution)/shard_map/all_to_all | solution.py:132
  171.8 11.7 %all-to-all-done.1 = f32[401,128,1]{0,2,1:T(1,128)} async-done(((f32[401,128,1]{0,2,1:T(1,128)}), f32[401,128,1]{0,2,1:T(1,128)}, u32[]{:S(2)}, u32[]{:S(2)}) %all-to-all-start.1) | async-done | bytes 205344 | tf_op jit(solution)/shard_map/all_to_all | solution.py:132
  183.5 1.1 copy.167
  185.6 1.2 multiply_reduce_fusion.3
  186.8 1.0 fusion.31
  187.8 2.0 multiply_convert_fusion.1
  189.8 2.9 multiply_reduce_fusion.6
  192.6 2.3 convolution_add_fusion.1
  195.0 1.0 add_convert_fusion.3
  196.0 1.6 fusion.2
  197.9 2.7 slice_reduce_fusion.128
  200.8 1.3 convolution_convert_fusion.1
  202.4 264.1 %all-reduce.4.cloned.1.call-done = f32[400,768]{1,0:T(8,128)} async-done(((f32[400,768]{1,0:T(8,128)}), f32[400,768]{1,0:T(8,128)}) %all-reduce.4.cloned.1.call-update) | async-done | bytes 1228816 | tf_op jit(solution)/shard_map/psum | solution.py:95
  466.5 1.5 multiply_reduce_fusion.1
  469.6 1.2 multiply_reduce_fusion.2
  470.9 1.0 fusion.32
  471.8 2.0 multiply_convert_fusion
  473.8 3.0 multiply_reduce_fusion.4
  476.8 2.4 convolution_add_fusion
  479.3 1.3 add_convert_fusion
  481.5 9.5 %all-to-all-start.2 = ((f32[401,128,1]{0,2,1:T(1,128)}), f32[401,128,1]{0,2,1:T(1,128)S(1)}, u32[]{:S(2)}, u32[]{:S(2)}) async-start(f32[401,128,1]{0,2,1:T(1,128)} %copy.161), calls=%async_computation.2 | async-start | bytes 524288 | tf_op jit(solution)/shard_map/all_to_all | solution.py:158
  491.1 2.6 fusion
  493.7 1.0 multiply_reduce_fusion.5
  495.2 8.9 %all-to-all-done.2 = f32[401,128,1]{0,2,1:T(1,128)S(1)} async-done(((f32[401,128,1]{0,2,1:T(1,128)}), f32[401,128,1]{0,2,1:T(1,128)S(1)}, u32[]{:S(2)}, u32[]{:S(2)}) %all-to-all-start.2) | async-done | bytes 205344 | tf_op jit(solution)/shard_map/all_to_all | solution.py:158
  505.0 1.0 copy.164
  506.0 7.7 all-to-all-start.3
  513.8 1.7 divide_subtract_fusion.3
  515.4 260.2 %all-reduce.6.cloned.1.call-done = f32[400,768]{1,0:T(8,128)} async-done(((f32[400,768]{1,0:T(8,128)}), f32[400,768]{1,0:T(8,128)}) %all-reduce.6.cloned.1.call-update) | async-done | bytes 1228816 | tf_op jit(solution)/shard_map/psum | solution.py:95
  775.7 1.4 multiply_reduce_fusion
  777.8 2.3 collective-permute-start.1
  780.1 2.6 divide_subtract_fusion
  782.7 5.2 collective-permute-done.1
  (219 shorter events, 87.7 us)
Async XLA Ops:
  8.1 36.8 %collective-permute-start = (f32[401,128]{1,0:T(8,128)S(1)}, f32[401,128]{1,0:T(8,128)S(1)}, u32[]{:S(2)}, u32[]{:S(2)}) collective-permute-start(f32[401,128]{1,0:T(8,128)S(1)} %pad_maximum_fusion.2), channel_id=1, source_target_pairs={{0,1},{1,2},{2,3},{3,0},{4,5},{5,6},{6,7},{7,4},{8,9},{9,10},{10,1... | collective-permute-start | bytes 615944 | tf_op jit(solution)/shard_map/ppermute | solution.py:17
  61.8 85.9 %copy-start = (f32[400,768]{1,0:T(8,128)S(1)}, f32[400,768]{1,0:T(8,128)}, u32[]{:S(2)}) copy-start(f32[400,768]{1,0:T(8,128)} %param.18) | copy-start | bytes 3686404
  135.9 24.2 %all-to-all-start = ((f32[128,401,1,1]{1,3,2,0:T(1,128)}), f32[128,401,1,1]{1,3,2,0:T(1,128)S(1)}, u32[]{:S(2)}, u32[]{:S(2)}) async-start(f32[128,401,1,1]{1,3,2,0:T(1,128)} %constant_dynamic-update-slice_fusion), calls=%async_computation | async-start | bytes 524288 | tf_op jit(solution)/shard_map/all_to_all | solution.py:121
  161.9 21.6 %all-to-all-start.1 = ((f32[401,128,1]{0,2,1:T(1,128)}), f32[401,128,1]{0,2,1:T(1,128)}, u32[]{:S(2)}, u32[]{:S(2)}) async-start(f32[401,128,1]{0,2,1:T(1,128)} %copy.159), calls=%async_computation.1 | async-start | bytes 524288 | tf_op jit(solution)/shard_map/all_to_all | solution.py:132
  170.7 295.8 %all-reduce.4.cloned.1.call-start = ((), (), s32[]{:S(2)}) async-start(), calls=%async_computation.4 | async-start | bytes 2457600 | tf_op jit(solution)/shard_map/psum | solution.py:95
  184.6 1.0 copy-start.8
  185.0 2.8 copy-start.5
  196.0 1.6 copy-start.16
  197.6 3.1 copy-start.17
  197.6 3.2 copy-start.20
  197.6 4.5 copy-start.6
  197.9 4.2 copy-start.11
  202.1 265.9 %copy-start.19 = (f32[768]{0:T(1024)S(1)}, f32[768]{0:T(1024)}, u32[]{:S(2)}) copy-start(f32[768]{0:T(1024)} %param.19) | copy-start | bytes 9220
  466.5 1.7 copy-start.1
  468.8 0.9 copy-start.2
  469.6 2.2 copy-start.9
  469.6 2.2 copy-start.10
  469.6 2.2 copy-start.4
  476.8 2.4 copy-start.3
  479.3 1.3 copy-start.18
  480.6 10.5 %copy-start.15 = (bf16[200,512]{1,0:T(8,128)(2,1)S(1)}, bf16[200,512]{1,0:T(8,128)(2,1)}, u32[]{:S(2)}) copy-start(bf16[200,512]{1,0:T(8,128)(2,1)} %get-tuple-element.157) | copy-start | bytes 614404
  481.5 22.6 %all-to-all-start.2 = ((f32[401,128,1]{0,2,1:T(1,128)}), f32[401,128,1]{0,2,1:T(1,128)S(1)}, u32[]{:S(2)}, u32[]{:S(2)}) async-start(f32[401,128,1]{0,2,1:T(1,128)} %copy.161), calls=%async_computation.2 | async-start | bytes 524288 | tf_op jit(solution)/shard_map/all_to_all | solution.py:158
  491.1 284.6 %all-reduce.6.cloned.1.call-start = ((), (), s32[]{:S(2)}) async-start(), calls=%async_computation.5 | async-start | bytes 2457600 | tf_op jit(solution)/shard_map/psum | solution.py:95
  491.1 2.6 copy-start.13
  491.1 2.6 copy-start.14
  504.9 8.8 %copy-start.7 = (f32[400,128]{1,0:T(8,128)S(1)}, f32[400,128]{1,0:T(8,128)}, u32[]{:S(2)}) copy-start(f32[400,128]{1,0:T(8,128)} %param.14) | copy-start | bytes 614404
  504.9 8.8 %copy-start.12 = (f32[400,128]{1,0:T(8,128)S(1)}, f32[400,128]{1,0:T(8,128)}, u32[]{:S(2)}) copy-start(f32[400,128]{1,0:T(8,128)} %copy-done.11) | copy-start | bytes 614404
  506.0 271.7 %all-to-all-start.3 = ((f32[401,128,1]{0,2,1:T(1,128)}), f32[401,128,1]{0,2,1:T(1,128)S(1)}, u32[]{:S(2)}, u32[]{:S(2)}) async-start(f32[401,128,1]{0,2,1:T(1,128)} %copy.164), calls=%async_computation.3 | async-start | bytes 524288 | tf_op jit(solution)/shard_map/all_to_all | solution.py:163
  777.8 10.1 %collective-permute-start.1 = (f32[401,128]{1,0:T(8,128)S(1)}, f32[401,128]{1,0:T(8,128)S(1)}, u32[]{:S(2)}, u32[]{:S(2)}) collective-permute-start(f32[401,128]{1,0:T(8,128)S(1)} %bitcast.221), channel_id=1, source_target_pairs={{0,3},{1,0},{2,1},{3,2},{4,7},{5,4},{6,5},{7,6},{8,11},{9,8},{10,9... | collective-permute-start | bytes 615944 | tf_op jit(solution)/shard_map/ppermute | solution.py:17
Sparse Core Ops, SparseCore 0:
  197.7 268.7 all-reduce.3
  498.3 277.2 all-reduce.5
